TPU v7x, 32 devices: a whole 2x2x4 slice. The times are simulated.
32 devices in a mesh: seq: 16 (over z, x, core), branch: 2 (over y).
Axes of the slice: x: 2, y: 2, z: 4, core: 2. Of those that a mesh axis runs over, the one named last changes fastest.
Arguments:
- queries: bfloat16 [2, 896, 2560], P('branch', 'seq'), may hold values from -100 to 100
- keys_values: bfloat16 [2, 896, 2560], P(None, 'seq', 'branch'), may hold values from -10 to 10
- residual_in: bfloat16 [2, 896, 2560], P('branch', 'seq'), may hold values from -90 to 90
- cross_gain: bfloat16 [2560], replicated, may hold values from 0.099609375 to 1.8984375
- text_kv: bfloat16 [2, 2, 512, 2560], replicated, may hold values from -90 to 90
- prompt_ids: int32 [2, 512], replicated, may hold values from 0 to 256383
- word_align: int32 [512], replicated, may hold values from 0 to 511, as said below
Outputs:
- attended: bfloat16 [2, 896, 2560], P('branch', 'seq')
- result: bfloat16 [2, 896, 2560], P('branch', 'seq')
Inputs may be any that keep to these rules, and one draw needn't show every extreme that they name: `word_align`: a permutation of the 512 source positions.
All inputs are finite; a program needn't handle non-finite values.
Results may differ from a plain program's by a relative error of at most 0.019.
Values may be sent and summed in bfloat16 or wider, within the bound.
A program may use at most 128 MiB of HBM per device.

v0:
```python
import math

import jax
import jax.numpy as jnp
from jax import lax
from jax.sharding import PartitionSpec as P

HD = 128


def spread(value, axis, source):
    kept = jnp.where(lax.axis_index(axis) == source, value, 0).astype(value.dtype)
    return lax.psum(kept, axis)


def alignment(prompt_ids, word_align):
    text_len = word_align.shape[0]
    word_pairs = jnp.arange(text_len, dtype=jnp.int32)[:, None] == word_align[None, :]
    aligned_ids = jnp.sum(jnp.where(word_pairs, prompt_ids[0][:, None], 0), axis=0)
    same_word = prompt_ids[1] == aligned_ids
    selection = jnp.where(word_pairs & same_word[None, :], 1.0, 0.0).astype(jnp.bfloat16)
    keep_own = jnp.where(same_word, 0.0, 1.0).astype(jnp.float32)
    return (selection, keep_own)


def rows_by_rows(left, right):
    return lax.dot_general(
        left, right, (((1,), (1,)), ((), ())), preferred_element_type=jnp.float32
    )


def start_carry(head_count, tok_rows):
    return (
        jnp.full((tok_rows, head_count), -1e30, jnp.float32),
        jnp.zeros((tok_rows, head_count), jnp.float32),
        jnp.zeros((tok_rows, head_count, HD), jnp.float32),
    )


def fold_keys(carry, query_rows, piece):
    row_peak, weight_sum, summed = carry
    head_count = query_rows.shape[1] // HD
    score_scale = 1.0 / math.sqrt(HD)
    key_rows = piece[0]
    value_rows = piece[1]
    peaks = []
    totals = []
    products = []
    for head in range(head_count):
        lower = head * HD
        scores = (
            rows_by_rows(query_rows[:, lower : lower + HD], key_rows[:, lower : lower + HD])
            * score_scale
        )
        old_peak = row_peak[:, head]
        new_peak = jnp.maximum(old_peak, jnp.max(scores, axis=1))
        weights = jnp.exp(scores - new_peak[:, None])
        totals.append(jnp.sum(weights, axis=1))
        update = jnp.dot(
            weights.astype(jnp.bfloat16),
            value_rows[:, lower : lower + HD],
            preferred_element_type=jnp.float32,
        )
        products.append(update)
        peaks.append(new_peak)
    return (jnp.stack(peaks, axis=1), jnp.stack(totals, axis=1), jnp.stack(products, axis=1))


def finish_heads(carry):
    row_peak, weight_sum, summed = carry
    tok_rows, head_count = weight_sum.shape
    output = summed / weight_sum[:, :, None]
    return output.reshape(tok_rows, head_count * HD).astype(jnp.bfloat16)


def text_maps(cross_query, text_keys):
    head_count = cross_query.shape[1] // HD
    score_scale = 1.0 / math.sqrt(HD)
    maps = []
    for head in range(head_count):
        lower = head * HD
        scores = (
            rows_by_rows(cross_query[:, lower : lower + HD], text_keys[:, lower : lower + HD])
            * score_scale
        )
        row_peak = jnp.max(scores, axis=-1, keepdims=True)
        weights = jnp.exp(scores - row_peak)
        maps.append(weights / jnp.sum(weights, axis=-1, keepdims=True))
    return jnp.stack(maps)


def inject(source_maps, own_maps, selection, keep_own):
    picked = jnp.einsum("hqs,sj->hqj", source_maps, selection, preferred_element_type=jnp.float32)
    return (picked + own_maps * keep_own).astype(jnp.bfloat16)


def per_device(queries, keys_values, residual_in, cross_gain, text_kv, prompt_ids, word_align):
    tok_rows = queries.shape[1]
    width = queries.shape[2]
    head_count = width // HD
    mixed = lax.all_to_all(queries, "branch", split_axis=2, concat_axis=0, tiled=True)
    half_heads = head_count // 2
    query_rows = mixed.reshape(2 * tok_rows, half_heads * HD)
    carry = fold_keys(
        start_carry(half_heads, 2 * tok_rows),
        query_rows,
        lax.all_gather(keys_values, "seq", axis=1, tiled=True),
    )
    local_out = finish_heads(carry).reshape(2, tok_rows, half_heads * HD)
    attended = lax.all_to_all(local_out, "branch", split_axis=0, concat_axis=2, tiled=True)
    branch_index = lax.axis_index("branch")
    middle = residual_in[0].astype(jnp.float32) + attended[0].astype(jnp.float32)
    cross_query = (
        middle
        * lax.rsqrt(jnp.mean(middle * middle, axis=-1, keepdims=True) + 1e-06)
        * cross_gain.astype(jnp.float32)
    ).astype(jnp.bfloat16)
    own_keys = lax.dynamic_index_in_dim(text_kv[0], branch_index, 0, keepdims=False)
    own_values = lax.dynamic_index_in_dim(text_kv[1], branch_index, 0, keepdims=False)
    selection, keep_own = alignment(prompt_ids, word_align)
    own_maps = text_maps(cross_query, own_keys)
    source_maps = spread(own_maps.astype(jnp.bfloat16), "branch", 0)

    def edit_branch():
        return inject(source_maps, own_maps, selection, keep_own)

    def source_branch():
        return source_maps

    cross_maps = lax.cond(branch_index == 1, edit_branch, source_branch)
    pieces = []
    for head in range(head_count):
        lower = head * HD
        pieces.append(
            jnp.dot(
                cross_maps[head],
                own_values[:, lower : lower + HD],
                preferred_element_type=jnp.float32,
            )
        )
    cross_out = jnp.concatenate(pieces, axis=1)
    result = (middle + cross_out).astype(jnp.bfloat16)
    return (attended, result[None])


def solution(mesh):
    in_specs = (
        P("branch", "seq", None),
        P(None, "seq", "branch"),
        P("branch", "seq", None),
        P(),
        P(),
        P(),
        P(),
    )
    out_specs = (P("branch", "seq", None), P("branch", "seq", None))
    return jax.shard_map(
        per_device, mesh=mesh, in_specs=in_specs, out_specs=out_specs, check_vma=False
    )
```

profile of v0, /device:TPU:0, one launch (start us, length us, event | category | flops | bytes accessed | tf_op | source)
XLA Modules:
  0.0 171.1 jit_solution(5957431489611977443)
XLA Ops:
  7.9 2.4 %copy.16 = bf16[1,56,2560]{1,0,2:T(2,128)(2,1)S(1)} copy(bf16[1,56,2560]{2,1,0:T(8,128)(2,1)} %param.9) | data formatting | bytes 573440 | tf_op args[0]
  10.9 14.3 %reduce.2 = bf16[2560,56]{1,0:T(8,128)(2,1)S(1)} reduce(bf16[2560,1,56]{2,1,0:T(2,128)(2,1)S(1)} %bitcast.266, bf16[]{:T(256)} %broadcast.149), dimensions={1}, to_apply=%bitcast.263.reduce_sub_computation | reduce | bytes 573442
  25.1 1.9 %reshape.144 = bf16[2,2,35840]{2,1,0:T(2,128)(2,1)} reshape(bf16[2560,56]{1,0:T(8,128)(2,1)S(1)} %reduce.2) | data formatting | bytes 573440
  27.0 4.2 %all-to-all-start = ((bf16[2,2,35840]{2,1,0:T(2,128)(2,1)}), bf16[2,2,35840]{2,1,0:T(2,128)(2,1)S(1)}, u32[]{:S(2)}, u32[]{:S(2)}) async-start(bf16[2,2,35840]{2,1,0:T(2,128)(2,1)} %reshape.144), calls=%async_computation | async-start | bytes 573440 | tf_op jit(solution)/shard_map/all_to_all | solution.py:101
  31.2 8.7 %fusion.185 = (bf16[1,2,512,2560]{3,2,1,0:T(8,128)(2,1)}, bf16[1,2,512,2560]{3,2,1,0:T(8,128)(2,1)}) fusion(bf16[2,2,512,2560]{3,2,1,0:T(8,128)(2,1)} %param.13), kind=kLoop, calls=%fused_computation.333 | loop fusion | bytes 20971520 | tf_op jit(solution)/shard_map/slice | solution.py:118
  40.0 2.1 %reshape.145 = bf16[2560,1,56]{2,1,0:T(2,128)(2,1)S(1)} reshape(bf16[2,2,35840]{2,1,0:T(2,128)(2,1)S(1)} %all-to-all-done) | data formatting | bytes 573440
  42.9 22.6 %all-gather.2.cloned.1.call-done = bf16[2,896,1280]{2,1,0:T(8,128)(2,1)} async-done(((bf16[2,56,1280]{2,1,0:T(8,128)(2,1)}), bf16[2,896,1280]{2,1,0:T(8,128)(2,1)}) %all-gather.2.cloned.1.call-update) | async-done | bytes 4587536 | tf_op jit(solution)/shard_map/all_gather | solution.py:107
  65.5 2.6 %slice_bitcast_fusion.1 = (bf16[896,1280]{1,0:T(8,128)(2,1)S(1)}, bf16[896,1280]{1,0:T(8,128)(2,1)S(1)}) fusion(bf16[2,896,1280]{2,1,0:T(8,128)(2,1)} %all-gather.2.cloned.1.call-done), kind=kLoop, calls=%fused_computation.6 | loop fusion | bytes 9175040 | tf_op jit(solution)/shard_map/squeeze | solution.py:44
  77.9 3.4 %all-to-all-start.1 = ((bf16[2,56,1280]{2,1,0:T(8,128)(2,1)}), bf16[2,56,1280]{2,1,0:T(8,128)(2,1)S(1)}, u32[]{:S(2)}, u32[]{:S(2)}) async-start(bf16[2,56,1280]{2,1,0:T(8,128)(2,1)} %convert_element_type.96), calls=%async_computation.1 | async-start | bytes 573440 | tf_op jit(solution)/shard_map/all_to_all | solution.py:110
  81.6 1.9 %dynamic-slice_bitcast_fusion.1 = bf16[512,2560]{1,0:T(8,128)(2,1)S(1)} fusion(bf16[1,2,512,2560]{3,2,1,0:T(8,128)(2,1)} %get-tuple-element.28, s32[]{:T(128)S(6)} %select_n.27), kind=kLoop, calls=%fused_computation.4 | loop fusion | bytes 5242884 | tf_op jit(solution)/shard_map/jit(dynamic_index_in_dim)/squeeze | solution.py:118
  83.6 3.9 %all-to-all-done.1 = bf16[2,56,1280]{2,1,0:T(8,128)(2,1)S(1)} async-done(((bf16[2,56,1280]{2,1,0:T(8,128)(2,1)}), bf16[2,56,1280]{2,1,0:T(8,128)(2,1)S(1)}, u32[]{:S(2)}, u32[]{:S(2)}) %all-to-all-start.1) | async-done | bytes 286752 | tf_op jit(solution)/shard_map/all_to_all | solution.py:110
  100.4 1.1 convert_select_fusion
  102.9 3.4 %dynamic-slice_bitcast_fusion = bf16[512,2560]{1,0:T(8,128)(2,1)} fusion(bf16[1,2,512,2560]{3,2,1,0:T(8,128)(2,1)} %get-tuple-element.29, s32[]{:T(128)S(6)} %select_n.27), kind=kLoop, calls=%fused_computation.3 | loop fusion | bytes 5242884 | tf_op jit(solution)/shard_map/jit(dynamic_index_in_dim)/squeeze | solution.py:119
  106.4 35.2 %all-reduce.2.cloned.1.call-done = bf16[20,56,512]{2,1,0:T(8,128)(2,1)} async-done(((bf16[20,56,512]{2,1,0:T(8,128)(2,1)}), bf16[20,56,512]{2,1,0:T(8,128)(2,1)}) %all-reduce.2.cloned.1.call-update) | async-done | bytes 1146896 | tf_op jit(solution)/shard_map/psum | solution.py:13
  142.6 1.1 fusion.29
  144.8 1.1 fusion.27
  148.1 1.1 fusion.24
  149.2 1.1 fusion.23
  151.4 1.1 fusion.21
  152.5 1.1 fusion.20
  154.7 1.1 fusion.18
  155.8 1.1 fusion.17
  158.0 1.1 fusion.15
  161.3 1.1 fusion.12
  (147 shorter events, 37.8 us)
Async XLA Ops:
  7.2 58.4 %all-gather.2.cloned.1.call-start = ((), (), s32[]{:S(2)}) async-start(), calls=%async_computation.2 | async-start | bytes 4874240 | tf_op jit(solution)/shard_map/all_gather | solution.py:107
  27.0 12.9 %all-to-all-start = ((bf16[2,2,35840]{2,1,0:T(2,128)(2,1)}), bf16[2,2,35840]{2,1,0:T(2,128)(2,1)S(1)}, u32[]{:S(2)}, u32[]{:S(2)}) async-start(bf16[2,2,35840]{2,1,0:T(2,128)(2,1)} %reshape.144), calls=%async_computation | async-start | bytes 573440 | tf_op jit(solution)/shard_map/all_to_all | solution.py:101
  77.9 9.6 %all-to-all-start.1 = ((bf16[2,56,1280]{2,1,0:T(8,128)(2,1)}), bf16[2,56,1280]{2,1,0:T(8,128)(2,1)S(1)}, u32[]{:S(2)}, u32[]{:S(2)}) async-start(bf16[2,56,1280]{2,1,0:T(8,128)(2,1)} %convert_element_type.96), calls=%async_computation.1 | async-start | bytes 573440 | tf_op jit(solution)/shard_map/all_to_all | solution.py:110
  81.3 60.2 %all-reduce.2.cloned.1.call-start = ((), (), s32[]{:S(2)}) async-start(), calls=%async_computation.3 | async-start | bytes 2293760 | tf_op jit(solution)/shard_map/psum | solution.py:13
  81.6 2.0 %copy-start.5 = (bf16[2560]{0:T(1024)(128)(2,1)S(1)}, bf16[2560]{0:T(1024)(128)(2,1)}, u32[]{:S(2)}) copy-start(bf16[2560]{0:T(1024)(128)(2,1)} %param.12) | copy-start | bytes 15364
  83.5 4.3 %copy-start = (bf16[1,56,2560]{2,1,0:T(8,128)(2,1)S(1)}, bf16[1,56,2560]{2,1,0:T(8,128)(2,1)}, u32[]{:S(2)}) copy-start(bf16[1,56,2560]{2,1,0:T(8,128)(2,1)} %param.11) | copy-start | bytes 860164
  100.4 1.2 copy-start.3
  100.4 1.2 copy-start.4
  106.4 57.1 %copy-start.2 = (bf16[1,2,7,8,1280]{4,3,1,2,0:T(8,128)(2,1)}, bf16[1,2,7,8,1280]{4,3,1,2,0:T(8,128)(2,1)S(1)}, u32[]{:S(2)}) copy-start(bf16[1,2,7,8,1280]{4,3,1,2,0:T(8,128)(2,1)S(1)} %copy.22) | copy-start | bytes 860164
Sparse Core Ops, SparseCore 0:
  10.2 55.2 all-gather.1
  101.7 39.7 all-reduce.1
where the time goes:
time: 173 us; the launch traced here: 171 us
  waiting for transfers between devices  62.3 us (36%)
  matrix products  34.2 us (20%)
  other arithmetic  26.2 us (15%)
  local copies, waits for them, and re-layouts  25.9 us (15%)
  between operations  14.6 us (8%)
  starting transfers between devices  7.98 us (5%)
    psum x1, waiting for transfers between devices, spread(): return lax.psum(kept, axis)  35.2 us
    all_gather x1, waiting for transfers between devices, per_device(): lax.all_gather(keys_values, 'seq', axis=1, tiled=True)  22.6 us
    dot_general x20, matrix products, per_device(): jnp.dot(cross_maps[head], own_values[:, lower:lower + HD], preferred_elem...  21.9 us
    unnamed x20, other arithmetic  16.1 us
    dot_general x30, matrix products, rows_by_rows(): lax.dot_general(left, right, (((1,), (1,)), ((), ())), preferred_element_...  9.3 us
    slice x1, local copies, waits for them, and re-layouts, per_device(): text_kv[0]  8.7 us
    unnamed x15, local copies, waits for them, and re-layouts  6.97 us
    all_to_all x1, starting transfers between devices, per_device(): lax.all_to_all(queries, 'branch', split_axis=2, concat_axis=0, tiled=True)  4.23 us
  transfers between devices with their start and end apart: 4, of which 3 were waited for; matrix products, arithmetic and copies ran while one was open for 22% of the time, Pallas kernels for 0%

commit v1 on v0

v1 whole, which is shorter than its diff:
```python
import functools
import math

import jax
import jax.numpy as jnp
from jax import lax
from jax.experimental import pallas as pl
from jax.experimental.pallas import tpu as pltpu
from jax.sharding import PartitionSpec as P

HD = 128
PAIR = 2
MESH = pl.DeviceIdType.MESH


def rows_by_rows(left, right):
    return lax.dot_general(
        left, right, (((1,), (1,)), ((), ())), preferred_element_type=jnp.float32
    )


def kernel(
    n,
    q_ref,
    kv_ref,
    res_ref,
    gain_ref,
    text_ref,
    ids_ref,
    align_ref,
    att_ref,
    out_ref,
    q_all,
    r_all,
    kv_all,
    text,
    moved,
    place,
    probs,
    totals,
    att,
    mid,
    squares,
    out,
    text_sem,
    own_sem,
    own_out_sem,
    recv_sem,
    send_z,
    send_x,
    send_c,
    y_send,
    y_recv,
    back_send,
    back_recv,
):
    rows = q_ref.shape[0]
    half = kv_ref.shape[2]
    heads = half // HD
    pairs = heads // PAIR
    wide = PAIR * HD
    text_len = text_ref.shape[2]
    tall = n // 4
    scale = 1.0 / math.sqrt(HD)
    me = lax.axis_index("seq")
    branch = lax.axis_index("branch")
    other = 1 - branch
    core = me % 2
    side = (me // 2) % 2
    level = me // 4
    mine = pl.multiple_of(branch * half, HD)
    theirs = pl.multiple_of(other * half, HD)

    def index(lev, sid, cor):
        return lev * 4 + sid * 2 + cor

    x_peer = index(level, 1 - side, core)
    c_peer = index(level, side, 1 - core)

    def text_copy(i):
        return pltpu.make_async_copy(
            text_ref.at[i // 2, i % 2, :, pl.ds(mine, half)], text.at[i], text_sem.at[i]
        )

    for i in range(4):
        text_copy(i).start()

    def own_copy(i):
        if i == 0:
            return pltpu.make_async_copy(
                q_ref.at[:, pl.ds(mine, half)], q_all.at[branch], own_sem.at[0]
            )
        if i == 1:
            return pltpu.make_async_copy(
                res_ref.at[:, pl.ds(mine, half)], r_all.at[branch], own_sem.at[1]
            )
        return pltpu.make_async_copy(kv_ref.at[i - 2], kv_all.at[me, i - 2], own_sem.at[i])

    for i in range(4):
        own_copy(i).start()

    barrier = pltpu.get_barrier_semaphore()

    def greet(seq, bra):
        pl.semaphore_signal(barrier, inc=1, device_id=(seq, bra), device_id_type=MESH)

    def z_peer(step):
        return index((level + step) % tall, side, core)

    @pl.loop(1, tall)
    def _(step):
        greet(z_peer(step), branch)

    greet(x_peer, branch)
    greet(c_peer, branch)
    greet(me, other)
    pl.semaphore_wait(barrier, tall + 2)

    def kv_copy(source, origin, which, peer, sem):
        return pltpu.make_async_remote_copy(
            src_ref=source,
            dst_ref=kv_all.at[origin, which],
            send_sem=sem,
            recv_sem=recv_sem.at[origin, which],
            device_id=(peer, branch),
            device_id_type=MESH,
        )

    def to_z(step, which):
        return kv_copy(kv_ref.at[which], me, which, z_peer(step), send_z.at[step, which])

    def to_x(lev, which, own):
        origin = index(lev, side, core)
        source = kv_ref.at[which] if own else kv_all.at[origin, which]
        return kv_copy(source, origin, which, x_peer, send_x.at[lev, which])

    def to_c(lev, sid, which, own):
        origin = index(lev, sid, core)
        source = kv_ref.at[which] if own else kv_all.at[origin, which]
        return kv_copy(source, origin, which, c_peer, send_c.at[lev * 2 + sid, which])

    def arrived(origin, which):
        pltpu.make_async_remote_copy(
            src_ref=kv_all.at[origin, which],
            dst_ref=kv_all.at[origin, which],
            send_sem=send_x.at[0, which],
            recv_sem=recv_sem.at[origin, which],
            device_id=(x_peer, branch),
            device_id_type=MESH,
        ).wait_recv()

    def y_copy(i):
        source, target = ((q_ref, q_all), (res_ref, r_all))[i]
        return pltpu.make_async_remote_copy(
            src_ref=source.at[:, pl.ds(theirs, half)],
            dst_ref=target.at[branch],
            send_sem=y_send.at[i],
            recv_sem=y_recv.at[i],
            device_id=(me, other),
            device_id_type=MESH,
        )

    def send_own(which):
        to_x(level, which, True).start()

        @pl.loop(1, tall)
        def _(step):
            to_z(step, which).start()

        to_c(level, side, which, True).start()

    send_own(0)
    y_copy(0).start()
    send_own(1)
    y_copy(1).start()

    align = align_ref[...]
    chosen = lax.broadcasted_iota(jnp.int32, (text_len, text_len), 0) == align
    place[...] = jnp.where(chosen, 1.0, 0.0).astype(jnp.bfloat16)
    edit_ids = ids_ref[1:2, :]
    row = lax.broadcasted_iota(jnp.int32, (16, text_len), 0)
    digits = jnp.where(
        row == 0,
        edit_ids >> 16,
        jnp.where(row == 1, (edit_ids >> 8) & 255, jnp.where(row == 2, edit_ids & 255, 0)),
    )
    digits = rows_by_rows(digits.astype(jnp.float32).astype(jnp.bfloat16), place[...])
    moved_ids = digits[0:1, :] * 65536.0 + digits[1:2, :] * 256.0 + digits[2:3, :]
    same = jnp.where(moved_ids == ids_ref[0:1, :].astype(jnp.float32), 1.0, 0.0)

    for i in range(4):
        text_copy(i).wait()

    def columns(pair):
        return pl.ds(pl.multiple_of(pair * wide, wide), wide)

    @pl.loop(0, pairs)
    def _(pair):
        for i in range(2):
            moved[i, :, columns(pair)] = jnp.dot(
                place[...], text[2 * i + 1, :, columns(pair)], preferred_element_type=jnp.float32
            ).astype(jnp.bfloat16)

    def pass_on(step, which):
        lev = (level + step) % tall
        arrived(index(lev, side, core), which)
        to_x(lev, which, False).start()
        to_c(lev, side, which, False).start()

    def pass_core(step, which):
        lev = (level + step) % tall
        arrived(index(lev, 1 - side, core), which)
        to_c(lev, 1 - side, which, False).start()

    def from_core(which):
        @pl.loop(0, 2 * tall)
        def _(i):
            arrived(index(i // 2, i % 2, 1 - core), which)

    @pl.loop(1, tall)
    def _(step):
        pass_on(step, 0)
        pass_core(step - 1, 0)

    pass_core(tall - 1, 0)
    own_copy(0).wait()
    own_copy(2).wait()
    y_copy(0).wait_recv()
    from_core(0)

    def head_columns(pair, i):
        return pl.ds(pl.multiple_of(pair * wide + i * HD, HD), HD)

    def joined(value):
        flat = value.astype(jnp.float32).reshape(value.shape[0] * value.shape[1], HD)
        return flat.astype(jnp.bfloat16)

    def weigh(pair):
        for i in range(PAIR):
            at = head_columns(pair, i)
            scores = rows_by_rows(joined(q_all[:, :, at]), joined(kv_all[:, 0, :, at]))
            peak = jnp.max(scores, axis=1, keepdims=True)
            weights = jnp.exp((scores - peak) * scale)
            total = jnp.sum(weights, axis=1, keepdims=True)
            probs[pair * PAIR + i] = weights.astype(jnp.bfloat16)
            totals[pair * PAIR + i] = jnp.broadcast_to(total, (2 * rows, HD))

    @pl.loop(1, tall)
    def _(step):
        pass_on(step, 1)
        pass_core(step - 1, 1)

        @pl.loop((step - 1) * pairs // (tall - 1), step * pairs // (tall - 1))
        def _(pair):
            weigh(pair)

    pass_core(tall - 1, 1)
    own_copy(1).wait()
    own_copy(3).wait()
    y_copy(1).wait_recv()
    from_core(1)

    def back_copy(which, pair):
        source, target = ((att, att_ref), (out, out_ref))[which]
        return pltpu.make_async_remote_copy(
            src_ref=source.at[other, :, columns(pair)],
            dst_ref=target.at[:, pl.ds(pl.multiple_of(mine + pair * wide, HD), wide)],
            send_sem=back_send.at[which, pair],
            recv_sem=back_recv.at[which, pair],
            device_id=(me, other),
            device_id_type=MESH,
        )

    def own_out(which, pair):
        source, target = ((att, att_ref), (out, out_ref))[which]
        return pltpu.make_async_copy(
            source.at[branch, :, columns(pair)],
            target.at[:, pl.ds(pl.multiple_of(mine + pair * wide, HD), wide)],
            own_out_sem.at[which, pair],
        )

    squares[0] = jnp.zeros((2 * rows, HD), jnp.float32)

    @pl.loop(0, pairs)
    def _(pair):
        added = squares[0]
        for i in range(PAIR):
            at = head_columns(pair, i)
            summed = jnp.dot(
                probs[pair * PAIR + i],
                joined(kv_all[:, 1, :, at]),
                preferred_element_type=jnp.float32,
            )
            rounded = (summed / totals[pair * PAIR + i]).reshape(2, rows, HD).astype(jnp.bfloat16)
            att[:, :, at] = rounded
            middle = r_all[:, :, at].astype(jnp.float32) + rounded.astype(jnp.float32)
            mid[:, :, at] = middle
            middle = middle.reshape(2 * rows, HD)
            added = added + middle * middle
        squares[0] = added
        back_copy(0, pair).start()
        own_out(0, pair).start()

    squares[0] = jnp.broadcast_to(
        jnp.sum(squares[0], axis=1, keepdims=True), (2 * rows, HD)
    )
    square_copy = pltpu.make_async_remote_copy(
        src_ref=squares.at[0],
        dst_ref=squares.at[1],
        send_sem=y_send.at[2],
        recv_sem=y_recv.at[2],
        device_id=(me, other),
        device_id_type=MESH,
    )
    square_copy.start()
    square_copy.wait_recv()
    norm = lax.rsqrt((squares[0] + squares[1]) * (1.0 / (2 * half)) + 1e-06)
    squares[2] = norm

    def text_map(query, keys):
        scores = rows_by_rows(query, keys)
        weights = jnp.exp((scores - jnp.max(scores, axis=1, keepdims=True)) * scale)
        return weights / jnp.sum(weights, axis=1, keepdims=True)

    @pl.loop(0, pairs)
    def _(pair):
        for i in range(PAIR):
            at = head_columns(pair, i)
            gain = gain_ref[:, pl.ds(pl.multiple_of(mine + pair * wide + i * HD, HD), HD)]
            middle = mid[:, :, at]
            query = middle.reshape(2 * rows, HD) * squares[2] * gain.astype(jnp.float32)
            query = query.reshape(2, rows, HD).astype(jnp.bfloat16)
            source_map = text_map(query[0], text[0, :, at])
            edit_map = text_map(query[1], moved[0, :, at])
            injected = jnp.where(same > 0.5, source_map, edit_map)
            source_out = jnp.dot(
                source_map.astype(jnp.bfloat16),
                text[2, :, at],
                preferred_element_type=jnp.float32,
            )
            edit_out = jnp.dot(
                injected.astype(jnp.bfloat16),
                moved[1, :, at],
                preferred_element_type=jnp.float32,
            )
            out[0, :, at] = (middle[0] + source_out).astype(jnp.bfloat16)
            out[1, :, at] = (middle[1] + edit_out).astype(jnp.bfloat16)
        back_copy(1, pair).start()
        own_out(1, pair).start()

    for which in range(2):

        @pl.loop(0, pairs)
        def _(pair):
            back_copy(which, pair).wait()
            own_out(which, pair).wait()

        y_copy(which).wait_send()
        to_x(level, which, True).wait_send()
        to_c(level, side, which, True).wait_send()
        to_c(level, 1 - side, which, False).wait_send()

        @pl.loop(1, tall)
        def _(step):
            lev = (level + step) % tall
            to_z(step, which).wait_send()
            to_x(lev, which, False).wait_send()
            to_c(lev, side, which, False).wait_send()
            to_c(lev, 1 - side, which, False).wait_send()

    square_copy.wait_send()


def per_device(n, queries, keys_values, residual_in, cross_gain, text_kv, prompt_ids, word_align):
    rows, width = queries.shape[1:]
    half = keys_values.shape[2]
    heads = half // HD
    pairs = heads // PAIR
    text_len = word_align.shape[0]
    keys = n * rows
    tall = n // 4
    vmem = pl.BlockSpec(memory_space=pltpu.VMEM)
    hbm = pl.BlockSpec(memory_space=pl.ANY)
    shape = jax.ShapeDtypeStruct((rows, width), jnp.bfloat16)
    bf16, f32 = jnp.bfloat16, jnp.float32
    dma = pltpu.SemaphoreType.DMA
    attended, result = pl.pallas_call(
        functools.partial(kernel, n),
        out_shape=(shape, shape),
        in_specs=[vmem, vmem, vmem, vmem, hbm, vmem, vmem],
        out_specs=(hbm, hbm),
        scratch_shapes=[
            pltpu.VMEM((2, rows, half), bf16),
            pltpu.VMEM((2, rows, half), bf16),
            pltpu.VMEM((n, 2, rows, half), bf16),
            pltpu.VMEM((4, text_len, half), bf16),
            pltpu.VMEM((2, text_len, half), bf16),
            pltpu.VMEM((text_len, text_len), bf16),
            pltpu.VMEM((heads, 2 * rows, keys), bf16),
            pltpu.VMEM((heads, 2 * rows, HD), f32),
            pltpu.VMEM((2, rows, half), bf16),
            pltpu.VMEM((2, rows, half), f32),
            pltpu.VMEM((3, 2 * rows, HD), f32),
            pltpu.VMEM((2, rows, half), bf16),
            dma((4,)),
            dma((4,)),
            dma((2, pairs)),
            dma((n, 2)),
            dma((tall, 2)),
            dma((tall, 2)),
            dma((2 * tall, 2)),
            dma((3,)),
            dma((3,)),
            dma((2, pairs)),
            dma((2, pairs)),
        ],
        compiler_params=pltpu.CompilerParams(
            collective_id=0, has_side_effects=True, vmem_limit_bytes=60 * 2**20
        ),
    )(
        queries[0],
        keys_values,
        residual_in[0],
        cross_gain[None],
        text_kv,
        prompt_ids,
        word_align[None],
    )
    return (attended[None], result[None])


def solution(mesh):
    in_specs = (
        P("branch", "seq", None),
        P(None, "seq", "branch"),
        P("branch", "seq", None),
        P(),
        P(),
        P(),
        P(),
    )
    out_specs = (P("branch", "seq", None), P("branch", "seq", None))
    return jax.shard_map(
        functools.partial(per_device, mesh.shape["seq"]),
        mesh=mesh,
        in_specs=in_specs,
        out_specs=out_specs,
        check_vma=False,
    )
```

time: 173 us -> 68.1 us (0.39)
  the two profiles are of different devices: /device:TPU:0 before, /device:TPU:8 now
where the time goes in v1:
time: 68.1 us; the launch traced here: 67.9 us
  Pallas kernels  62.6 us (92%)
  local copies, waits for them, and re-layouts  4.67 us (7%)
    pallas_call x1, Pallas kernels, per_device(): pl.pallas_call(functools.partial(kernel, n), out_shape=(shape, shape), in...  62.6 us
    unnamed x2, local copies, waits for them, and re-layouts  3.38 us

profile of v1, /device:TPU:8, one launch (start us, length us, event | category | flops | bytes accessed | tf_op | source)
XLA Modules:
  0.0 67.9 jit_solution(18381896316148033170)
XLA Ops:
  0.6 1.3 %broadcast_in_dim.12.gain_ref = bf16[1,2560]{1,0:T(2,128)(2,1)} reshape(bf16[2560]{0:T(1024)(128)(2,1)} %param.10) | data formatting | bytes 10240 | tf_op jit(solution)/shard_map/broadcast_in_dim | solution.py:424
  1.9 62.6 %shard_map.86 = (bf16[56,2560]{1,0:T(8,128)(2,1)}, bf16[56,2560]{1,0:T(8,128)(2,1)}) custom-call(bf16[56,2560]{1,0:T(8,128)(2,1)} %bitcast.5, bf16[2,56,1280]{2,1,0:T(8,128)(2,1)} %kv_ref.1, bf16[56,2560]{1,0:T(8,128)(2,1)} %bitcast.6, bf16[1,2560]{1,0:T(2,128)(2,1)} %broadcast_in_dim.12.gain_ref, bf16[2,2,512,2560]{3,2,1,0:T(8,128)(2,1)} %text_ref.1, ...), custom_call_target="tpu_custom_call" | custom-call | tf_op jit(solution)/shard_map/pallas_call | solution.py:387
  64.5 1.7 %copy.11 = bf16[1,56,2560]{2,1,0:T(8,128)(2,1)} copy(bf16[1,56,2560]{2,1,0:T(8,128)(2,1)} %bitcast.8) | data formatting | bytes 573440
  66.2 1.7 %copy.12 = bf16[1,56,2560]{2,1,0:T(8,128)(2,1)} copy(bf16[1,56,2560]{2,1,0:T(8,128)(2,1)} %bitcast.7) | data formatting | bytes 573440

commit v2 on v1

--- a/solution.py
+++ b/solution.py
@@ -46,7 +46,8 @@
     own_sem,
     own_out_sem,
     recv_sem,
-    send_z,
+    send_up,
+    send_down,
     send_x,
     send_c,
     y_send,
@@ -104,17 +105,23 @@
     def greet(seq, bra):
         pl.semaphore_signal(barrier, inc=1, device_id=(seq, bra), device_id_type=MESH)
 
-    def z_peer(step):
-        return index((level + step) % tall, side, core)
-
-    @pl.loop(1, tall)
-    def _(step):
-        greet(z_peer(step), branch)
+    has_above = level + 1 < tall
+    has_below = level > 0
+    above = index((level + 1) % tall, side, core)
+    below = index((level + tall - 1) % tall, side, core)
+
+    @pl.when(has_above)
+    def _():
+        greet(above, branch)
+
+    @pl.when(has_below)
+    def _():
+        greet(below, branch)
 
     greet(x_peer, branch)
     greet(c_peer, branch)
     greet(me, other)
-    pl.semaphore_wait(barrier, tall + 2)
+    pl.semaphore_wait(barrier, 3 + has_above.astype(jnp.int32) + has_below.astype(jnp.int32))
 
     def kv_copy(source, origin, which, peer, sem):
         return pltpu.make_async_remote_copy(
@@ -126,8 +133,15 @@
             device_id_type=MESH,
         )
 
-    def to_z(step, which):
-        return kv_copy(kv_ref.at[which], me, which, z_peer(step), send_z.at[step, which])
+    def to_above(lev, which, own):
+        origin = index(lev, side, core)
+        source = kv_ref.at[which] if own else kv_all.at[origin, which]
+        return kv_copy(source, origin, which, above, send_up.at[lev, which])
+
+    def to_below(lev, which, own):
+        origin = index(lev, side, core)
+        source = kv_ref.at[which] if own else kv_all.at[origin, which]
+        return kv_copy(source, origin, which, below, send_down.at[lev, which])
 
     def to_x(lev, which, own):
         origin = index(lev, side, core)
@@ -163,9 +177,13 @@
     def send_own(which):
         to_x(level, which, True).start()
 
-        @pl.loop(1, tall)
-        def _(step):
-            to_z(step, which).start()
+        @pl.when(has_above)
+        def _():
+            to_above(level, which, True).start()
+
+        @pl.when(has_below)
+        def _():
+            to_below(level, which, True).start()
 
         to_c(level, side, which, True).start()
 
@@ -194,23 +212,51 @@
     def columns(pair):
         return pl.ds(pl.multiple_of(pair * wide, wide), wide)
 
-    @pl.loop(0, pairs)
-    def _(pair):
+    def move(pair):
         for i in range(2):
             moved[i, :, columns(pair)] = jnp.dot(
                 place[...], text[2 * i + 1, :, columns(pair)], preferred_element_type=jnp.float32
             ).astype(jnp.bfloat16)
 
     def pass_on(step, which):
-        lev = (level + step) % tall
-        arrived(index(lev, side, core), which)
-        to_x(lev, which, False).start()
-        to_c(lev, side, which, False).start()
-
-    def pass_core(step, which):
-        lev = (level + step) % tall
+        low, high = level - step, level + step
+
+        @pl.when(low >= 0)
+        def _():
+            arrived(index(low, side, core), which)
+
+            @pl.when(has_above)
+            def _():
+                to_above(low, which, False).start()
+
+            to_x(low, which, False).start()
+            to_c(low, side, which, False).start()
+
+        @pl.when(high < tall)
+        def _():
+            arrived(index(high, side, core), which)
+
+            @pl.when(has_below)
+            def _():
+                to_below(high, which, False).start()
+
+            to_x(high, which, False).start()
+            to_c(high, side, which, False).start()
+
+    def across(lev, which):
         arrived(index(lev, 1 - side, core), which)
         to_c(lev, 1 - side, which, False).start()
+
+    def pass_core(step, which):
+        low, high = level - step, level + step
+
+        @pl.when(low >= 0)
+        def _():
+            across(low, which)
+
+        @pl.when(high < tall)
+        def _():
+            across(high, which)
 
     def from_core(which):
         @pl.loop(0, 2 * tall)
@@ -220,7 +266,18 @@
     @pl.loop(1, tall)
     def _(step):
         pass_on(step, 0)
-        pass_core(step - 1, 0)
+
+        @pl.when(step == 1)
+        def _():
+            across(level, 0)
+
+        @pl.when(step > 1)
+        def _():
+            pass_core(step - 1, 0)
+
+        @pl.loop((step - 1) * pairs // (tall - 1), step * pairs // (tall - 1))
+        def _(pair):
+            move(pair)
 
     pass_core(tall - 1, 0)
     own_copy(0).wait()
@@ -248,7 +305,14 @@
     @pl.loop(1, tall)
     def _(step):
         pass_on(step, 1)
-        pass_core(step - 1, 1)
+
+        @pl.when(step == 1)
+        def _():
+            across(level, 1)
+
+        @pl.when(step > 1)
+        def _():
+            pass_core(step - 1, 1)
 
         @pl.loop((step - 1) * pairs // (tall - 1), step * pairs // (tall - 1))
         def _(pair):
@@ -356,19 +420,37 @@
             own_out(which, pair).wait()
 
         y_copy(which).wait_send()
-        to_x(level, which, True).wait_send()
-        to_c(level, side, which, True).wait_send()
-        to_c(level, 1 - side, which, False).wait_send()
-
-        @pl.loop(1, tall)
-        def _(step):
-            lev = (level + step) % tall
-            to_z(step, which).wait_send()
+
+        @pl.loop(0, tall)
+        def _(lev):
             to_x(lev, which, False).wait_send()
-            to_c(lev, side, which, False).wait_send()
-            to_c(lev, 1 - side, which, False).wait_send()
+            to_c(lev, 0, which, False).wait_send()
+            to_c(lev, 1, which, False).wait_send()
+
+            @pl.when(jnp.logical_and(has_above, lev <= level))
+            def _():
+                to_above(lev, which, False).wait_send()
+
+            @pl.when(jnp.logical_and(has_below, lev >= level))
+            def _():
+                to_below(lev, which, False).wait_send()
 
     square_copy.wait_send()
+
+
+def copy_out(att_in, out_in, att_ref, out_ref, sem):
+    half = att_in.shape[1] // 2
+    copies = []
+    for i, (source, target) in enumerate(((att_in, att_ref), (out_in, out_ref))):
+        for j in range(2):
+            at = pl.ds(j * half, half)
+            copies.append(
+                pltpu.make_async_copy(source.at[:, at], target.at[:, at], sem.at[2 * i + j])
+            )
+    for copy in copies:
+        copy.start()
+    for copy in copies:
+        copy.wait()
 
 
 def per_device(n, queries, keys_values, residual_in, cross_gain, text_kv, prompt_ids, word_align):
@@ -408,6 +490,7 @@
             dma((n, 2)),
             dma((tall, 2)),
             dma((tall, 2)),
+            dma((tall, 2)),
             dma((2 * tall, 2)),
             dma((3,)),
             dma((3,)),
@@ -426,6 +509,13 @@
         prompt_ids,
         word_align[None],
     )
+    attended, result = pl.pallas_call(
+        copy_out,
+        out_shape=(shape, shape),
+        in_specs=[hbm, hbm],
+        out_specs=(hbm, hbm),
+        scratch_shapes=[dma((4,))],
+    )(attended, result)
     return (attended[None], result[None])
 
 

time: 68.1 us -> 73.7 us (1.082)
  the two profiles are of different devices: /device:TPU:8 before, /device:TPU:0 now
where the time goes in v2:
time: 73.7 us; the launch traced here: 73.5 us
  Pallas kernels  71.5 us (97%)
  local copies, waits for them, and re-layouts  1.3 us (2%)
    pallas_call x1, Pallas kernels, per_device(): pl.pallas_call(functools.partial(kernel, n), out_shape=(shape, shape), in...  53 us
    pallas_call x1, Pallas kernels, per_device(): pl.pallas_call(copy_out, out_shape=(shape, shape), in_specs=[hbm, hbm], o...  18.5 us

profile of v2, /device:TPU:0, one launch (start us, length us, event | category | flops | bytes accessed | tf_op | source)
XLA Modules:
  0.0 73.5 jit_solution(2320639243453076135)
XLA Ops:
  0.6 1.3 %broadcast_in_dim.12.gain_ref = bf16[1,2560]{1,0:T(2,128)(2,1)} reshape(bf16[2560]{0:T(1024)(128)(2,1)} %param.10) | data formatting | bytes 10240 | tf_op jit(solution)/shard_map/broadcast_in_dim | solution.py:507
  1.9 53.0 %shard_map.86 = (bf16[56,2560]{1,0:T(8,128)(2,1)}, bf16[56,2560]{1,0:T(8,128)(2,1)}) custom-call(bf16[56,2560]{1,0:T(8,128)(2,1)} %bitcast.5, bf16[2,56,1280]{2,1,0:T(8,128)(2,1)} %kv_ref.1, bf16[56,2560]{1,0:T(8,128)(2,1)} %bitcast.6, bf16[1,2560]{1,0:T(2,128)(2,1)} %broadcast_in_dim.12.gain_ref, bf16[2,2,512,2560]{3,2,1,0:T(8,128)(2,1)} %text_ref.1, ...), custom_call_target="tpu_custom_call" | custom-call | tf_op jit(solution)/shard_map/pallas_call | solution.py:469
  54.9 18.5 %shard_map.87 = (bf16[56,2560]{1,0:T(8,128)(2,1)}, bf16[56,2560]{1,0:T(8,128)(2,1)}) custom-call(bf16[56,2560]{1,0:T(8,128)(2,1)} %get-tuple-element.6.att_in, bf16[56,2560]{1,0:T(8,128)(2,1)} %get-tuple-element.7.out_in), custom_call_target="tpu_custom_call" | custom-call | tf_op jit(solution)/shard_map/pallas_call | solution.py:512

commit v3 on v2

--- a/solution.py
+++ b/solution.py
@@ -50,6 +50,7 @@
     send_down,
     send_x,
     send_c,
+    relay_sem,
     y_send,
     y_recv,
     back_send,
@@ -60,6 +61,8 @@
     heads = half // HD
     pairs = heads // PAIR
     wide = PAIR * HD
+    grouped = heads // 2 if heads % 2 == 0 else heads
+    groups = heads // grouped
     text_len = text_ref.shape[2]
     tall = n // 4
     scale = 1.0 / math.sqrt(HD)
@@ -218,6 +221,26 @@
                 place[...], text[2 * i + 1, :, columns(pair)], preferred_element_type=jnp.float32
             ).astype(jnp.bfloat16)
 
+    paired = level + 1 - 2 * (level % 2)
+    relieved = paired < tall
+
+    def relayed(lev, which):
+        return jnp.logical_and(lev == paired, relieved) if which == 1 else False
+
+    def forward_x(lev, which):
+        if which == 0:
+            to_x(lev, which, False).start()
+        else:
+
+            @pl.when(jnp.logical_not(relayed(lev, which)))
+            def _():
+                to_x(lev, which, False).start()
+
+    def to_paired():
+        origin = index(level, 1 - side, core)
+        peer = index(lax.rem(paired, tall), side, core)
+        return kv_copy(kv_all.at[origin, 1], origin, 1, peer, relay_sem.at[0])
+
     def pass_on(step, which):
         low, high = level - step, level + step
 
@@ -229,7 +252,7 @@
             def _():
                 to_above(low, which, False).start()
 
-            to_x(low, which, False).start()
+            forward_x(low, which)
             to_c(low, side, which, False).start()
 
         @pl.when(high < tall)
@@ -240,11 +263,17 @@
             def _():
                 to_below(high, which, False).start()
 
-            to_x(high, which, False).start()
+            forward_x(high, which)
             to_c(high, side, which, False).start()
 
     def across(lev, which):
         arrived(index(lev, 1 - side, core), which)
+        if which == 1 and lev is level:
+
+            @pl.when(relieved)
+            def _():
+                to_paired().start()
+
         to_c(lev, 1 - side, which, False).start()
 
     def pass_core(step, which):
@@ -263,21 +292,31 @@
         def _(i):
             arrived(index(i // 2, i % 2, 1 - core), which)
 
-    @pl.loop(1, tall)
-    def _(step):
-        pass_on(step, 0)
-
-        @pl.when(step == 1)
-        def _():
-            across(level, 0)
-
-        @pl.when(step > 1)
-        def _():
-            pass_core(step - 1, 0)
-
+    def moves(step):
         @pl.loop((step - 1) * pairs // (tall - 1), step * pairs // (tall - 1))
         def _(pair):
             move(pair)
+
+    def pass_core_or_own(step, which):
+        @pl.when(step == 0)
+        def _():
+            across(level, which)
+
+        @pl.when(step > 0)
+        def _():
+            pass_core(step, which)
+
+    pass_on(1, 0)
+    across(level, 0)
+    moves(1)
+
+    @pl.loop(2, tall)
+    def _(step):
+        pass_on(step, 0)
+        pass_core(step - 1, 0)
+        pass_on(step - 1, 1)
+        pass_core_or_own(step - 2, 1)
+        moves(step)
 
     pass_core(tall - 1, 0)
     own_copy(0).wait()
@@ -292,31 +331,24 @@
         flat = value.astype(jnp.float32).reshape(value.shape[0] * value.shape[1], HD)
         return flat.astype(jnp.bfloat16)
 
-    def weigh(pair):
-        for i in range(PAIR):
-            at = head_columns(pair, i)
+    def weigh(group):
+        for i in range(grouped):
+            head = group * grouped + i
+            at = pl.ds(pl.multiple_of(head * HD, HD), HD)
             scores = rows_by_rows(joined(q_all[:, :, at]), joined(kv_all[:, 0, :, at]))
             peak = jnp.max(scores, axis=1, keepdims=True)
             weights = jnp.exp((scores - peak) * scale)
             total = jnp.sum(weights, axis=1, keepdims=True)
-            probs[pair * PAIR + i] = weights.astype(jnp.bfloat16)
-            totals[pair * PAIR + i] = jnp.broadcast_to(total, (2 * rows, HD))
-
-    @pl.loop(1, tall)
-    def _(step):
-        pass_on(step, 1)
-
-        @pl.when(step == 1)
-        def _():
-            across(level, 1)
-
-        @pl.when(step > 1)
-        def _():
-            pass_core(step - 1, 1)
-
-        @pl.loop((step - 1) * pairs // (tall - 1), step * pairs // (tall - 1))
-        def _(pair):
-            weigh(pair)
+            probs[head] = weights.astype(jnp.bfloat16)
+            totals[head] = jnp.broadcast_to(total, (2 * rows, HD))
+
+    weigh(0)
+    pass_on(tall - 1, 1)
+    pass_core_or_own(tall - 2, 1)
+
+    @pl.loop(1, groups)
+    def _(group):
+        weigh(group)
 
     pass_core(tall - 1, 1)
     own_copy(1).wait()
@@ -324,46 +356,53 @@
     y_copy(1).wait_recv()
     from_core(1)
 
-    def back_copy(which, pair):
+    def span(which, part):
+        size = (grouped * HD, wide)[which]
+        return pl.multiple_of(part * size, HD), size
+
+    def back_copy(which, part):
         source, target = ((att, att_ref), (out, out_ref))[which]
+        start, size = span(which, part)
         return pltpu.make_async_remote_copy(
-            src_ref=source.at[other, :, columns(pair)],
-            dst_ref=target.at[:, pl.ds(pl.multiple_of(mine + pair * wide, HD), wide)],
-            send_sem=back_send.at[which, pair],
-            recv_sem=back_recv.at[which, pair],
+            src_ref=source.at[other, :, pl.ds(start, size)],
+            dst_ref=target.at[:, pl.ds(pl.multiple_of(mine + start, HD), size)],
+            send_sem=back_send.at[which, part],
+            recv_sem=back_recv.at[which, part],
             device_id=(me, other),
             device_id_type=MESH,
         )
 
-    def own_out(which, pair):
+    def own_out(which, part):
         source, target = ((att, att_ref), (out, out_ref))[which]
+        start, size = span(which, part)
         return pltpu.make_async_copy(
-            source.at[branch, :, columns(pair)],
-            target.at[:, pl.ds(pl.multiple_of(mine + pair * wide, HD), wide)],
-            own_out_sem.at[which, pair],
+            source.at[branch, :, pl.ds(start, size)],
+            target.at[:, pl.ds(pl.multiple_of(mine + start, HD), size)],
+            own_out_sem.at[which, part],
         )
 
     squares[0] = jnp.zeros((2 * rows, HD), jnp.float32)
 
-    @pl.loop(0, pairs)
-    def _(pair):
+    @pl.loop(0, groups)
+    def _(group):
         added = squares[0]
-        for i in range(PAIR):
-            at = head_columns(pair, i)
+        for i in range(grouped):
+            head = group * grouped + i
+            at = pl.ds(pl.multiple_of(head * HD, HD), HD)
             summed = jnp.dot(
-                probs[pair * PAIR + i],
+                probs[head],
                 joined(kv_all[:, 1, :, at]),
                 preferred_element_type=jnp.float32,
             )
-            rounded = (summed / totals[pair * PAIR + i]).reshape(2, rows, HD).astype(jnp.bfloat16)
+            rounded = (summed / totals[head]).reshape(2, rows, HD).astype(jnp.bfloat16)
             att[:, :, at] = rounded
             middle = r_all[:, :, at].astype(jnp.float32) + rounded.astype(jnp.float32)
             mid[:, :, at] = middle
             middle = middle.reshape(2 * rows, HD)
             added = added + middle * middle
         squares[0] = added
-        back_copy(0, pair).start()
-        own_out(0, pair).start()
+        back_copy(0, group).start()
+        own_out(0, group).start()
 
     squares[0] = jnp.broadcast_to(
         jnp.sum(squares[0], axis=1, keepdims=True), (2 * rows, HD)
@@ -414,16 +453,23 @@
 
     for which in range(2):
 
-        @pl.loop(0, pairs)
-        def _(pair):
-            back_copy(which, pair).wait()
-            own_out(which, pair).wait()
+        @pl.loop(0, (groups, pairs)[which])
+        def _(part):
+            back_copy(which, part).wait()
+            own_out(which, part).wait()
 
         y_copy(which).wait_send()
 
         @pl.loop(0, tall)
         def _(lev):
-            to_x(lev, which, False).wait_send()
+            if which == 0:
+                to_x(lev, which, False).wait_send()
+            else:
+
+                @pl.when(jnp.logical_not(relayed(lev, which)))
+                def _():
+                    to_x(lev, which, False).wait_send()
+
             to_c(lev, 0, which, False).wait_send()
             to_c(lev, 1, which, False).wait_send()
 
@@ -435,22 +481,16 @@
             def _():
                 to_below(lev, which, False).wait_send()
 
+    @pl.when(relieved)
+    def _():
+        to_paired().wait_send()
+
     square_copy.wait_send()
 
 
-def copy_out(att_in, out_in, att_ref, out_ref, sem):
-    half = att_in.shape[1] // 2
-    copies = []
-    for i, (source, target) in enumerate(((att_in, att_ref), (out_in, out_ref))):
-        for j in range(2):
-            at = pl.ds(j * half, half)
-            copies.append(
-                pltpu.make_async_copy(source.at[:, at], target.at[:, at], sem.at[2 * i + j])
-            )
-    for copy in copies:
-        copy.start()
-    for copy in copies:
-        copy.wait()
+def copy_out(att_in, out_in, att_ref, out_ref):
+    att_ref[...] = att_in[...]
+    out_ref[...] = out_in[...]
 
 
 def per_device(n, queries, keys_values, residual_in, cross_gain, text_kv, prompt_ids, word_align):
@@ -492,6 +532,7 @@
             dma((tall, 2)),
             dma((tall, 2)),
             dma((2 * tall, 2)),
+            dma((1,)),
             dma((3,)),
             dma((3,)),
             dma((2, pairs)),
@@ -512,9 +553,8 @@
     attended, result = pl.pallas_call(
         copy_out,
         out_shape=(shape, shape),
-        in_specs=[hbm, hbm],
-        out_specs=(hbm, hbm),
-        scratch_shapes=[dma((4,))],
+        in_specs=[vmem, vmem],
+        out_specs=(vmem, vmem),
     )(attended, result)
     return (attended[None], result[None])
 

time: 73.7 us -> 56.2 us (0.76)
  Pallas kernels: 71.5 us -> 54.1 us
    pallas_call x1, Pallas kernels: 18.5 us -> 1.87 us  [per_device(): pl.pallas_call(copy_out, out_shape=(shape, shape), in_specs=[vmem, vmem],...]
    pallas_call x1, Pallas kernels: 53 us -> 52.2 us  [per_device(): pl.pallas_call(functools.partial(kernel, n), out_shape=(shape, shape), in...]
where the time goes in v3:
time: 56.2 us; the launch traced here: 56 us
  Pallas kernels  54.1 us (96%)
  local copies, waits for them, and re-layouts  1.3 us (2%)
  between operations  0.64 us (1%)
    pallas_call x1, Pallas kernels, per_device(): pl.pallas_call(functools.partial(kernel, n), out_shape=(shape, shape), in...  52.2 us
    pallas_call x1, Pallas kernels, per_device(): pl.pallas_call(copy_out, out_shape=(shape, shape), in_specs=[vmem, vmem],...  1.87 us
    broadcast_in_dim x1, local copies, waits for them, and re-layouts, per_device(): cross_gain[None]  1.3 us

profile of v3, /device:TPU:0, one launch (start us, length us, event | category | flops | bytes accessed | tf_op | source)
XLA Modules:
  0.0 56.0 jit_solution(9553721992630683654)
XLA Ops:
  0.6 1.3 %broadcast_in_dim.12.gain_ref = bf16[1,2560]{1,0:T(2,128)(2,1)} reshape(bf16[2560]{0:T(1024)(128)(2,1)} %param.10) | data formatting | bytes 10240 | tf_op jit(solution)/shard_map/broadcast_in_dim | solution.py:548
  1.9 52.2 %shard_map.86 = (bf16[56,2560]{1,0:T(8,128)(2,1)}, bf16[56,2560]{1,0:T(8,128)(2,1)}) custom-call(bf16[56,2560]{1,0:T(8,128)(2,1)} %bitcast.5, bf16[2,56,1280]{2,1,0:T(8,128)(2,1)} %kv_ref.1, bf16[56,2560]{1,0:T(8,128)(2,1)} %bitcast.6, bf16[1,2560]{1,0:T(2,128)(2,1)} %broadcast_in_dim.12.gain_ref, bf16[2,2,512,2560]{3,2,1,0:T(8,128)(2,1)} %text_ref.1, ...), custom_call_target="tpu_custom_call" | custom-call | tf_op jit(solution)/shard_map/pallas_call | solution.py:509
  54.2 1.9 %shard_map.87 = (bf16[56,2560]{1,0:T(8,128)(2,1)}, bf16[56,2560]{1,0:T(8,128)(2,1)}) custom-call(bf16[56,2560]{1,0:T(8,128)(2,1)} %get-tuple-element.6.att_in, bf16[56,2560]{1,0:T(8,128)(2,1)} %get-tuple-element.7.out_in), custom_call_target="tpu_custom_call" | custom-call | tf_op jit(solution)/shard_map/pallas_call | solution.py:553

commit v4 on v3

--- a/solution.py
+++ b/solution.py
@@ -41,6 +41,7 @@
     att,
     mid,
     squares,
+    partial,
     out,
     text_sem,
     own_sem,
@@ -63,6 +64,8 @@
     wide = PAIR * HD
     grouped = heads // 2 if heads % 2 == 0 else heads
     groups = heads // grouped
+    part = grouped * HD
+    classes = 2 * groups
     text_len = text_ref.shape[2]
     tall = n // 4
     scale = 1.0 / math.sqrt(HD)
@@ -78,6 +81,9 @@
     def index(lev, sid, cor):
         return lev * 4 + sid * 2 + cor
 
+    def own_kv(which):
+        return kv_ref.at[which // groups, :, pl.ds(which % groups * part, part)]
+
     x_peer = index(level, 1 - side, core)
     c_peer = index(level, side, 1 - core)
 
@@ -98,9 +104,9 @@
             return pltpu.make_async_copy(
                 res_ref.at[:, pl.ds(mine, half)], r_all.at[branch], own_sem.at[1]
             )
-        return pltpu.make_async_copy(kv_ref.at[i - 2], kv_all.at[me, i - 2], own_sem.at[i])
-
-    for i in range(4):
+        return pltpu.make_async_copy(own_kv(i - 2), kv_all.at[me, i - 2], own_sem.at[i])
+
+    for i in range(2 + classes):
         own_copy(i).start()
 
     barrier = pltpu.get_barrier_semaphore()
@@ -138,22 +144,22 @@
 
     def to_above(lev, which, own):
         origin = index(lev, side, core)
-        source = kv_ref.at[which] if own else kv_all.at[origin, which]
+        source = own_kv(which) if own else kv_all.at[origin, which]
         return kv_copy(source, origin, which, above, send_up.at[lev, which])
 
     def to_below(lev, which, own):
         origin = index(lev, side, core)
-        source = kv_ref.at[which] if own else kv_all.at[origin, which]
+        source = own_kv(which) if own else kv_all.at[origin, which]
         return kv_copy(source, origin, which, below, send_down.at[lev, which])
 
     def to_x(lev, which, own):
         origin = index(lev, side, core)
-        source = kv_ref.at[which] if own else kv_all.at[origin, which]
+        source = own_kv(which) if own else kv_all.at[origin, which]
         return kv_copy(source, origin, which, x_peer, send_x.at[lev, which])
 
     def to_c(lev, sid, which, own):
         origin = index(lev, sid, core)
-        source = kv_ref.at[which] if own else kv_all.at[origin, which]
+        source = own_kv(which) if own else kv_all.at[origin, which]
         return kv_copy(source, origin, which, c_peer, send_c.at[lev * 2 + sid, which])
 
     def arrived(origin, which):
@@ -190,10 +196,10 @@
 
         to_c(level, side, which, True).start()
 
-    send_own(0)
-    y_copy(0).start()
-    send_own(1)
-    y_copy(1).start()
+    for which in range(classes):
+        send_own(which)
+        if which < 2:
+            y_copy(which).start()
 
     align = align_ref[...]
     chosen = lax.broadcasted_iota(jnp.int32, (text_len, text_len), 0) == align
@@ -225,10 +231,10 @@
     relieved = paired < tall
 
     def relayed(lev, which):
-        return jnp.logical_and(lev == paired, relieved) if which == 1 else False
+        return jnp.logical_and(lev == paired, relieved) if which >= groups else False
 
     def forward_x(lev, which):
-        if which == 0:
+        if which < groups:
             to_x(lev, which, False).start()
         else:
 
@@ -236,10 +242,10 @@
             def _():
                 to_x(lev, which, False).start()
 
-    def to_paired():
+    def to_paired(which):
         origin = index(level, 1 - side, core)
         peer = index(lax.rem(paired, tall), side, core)
-        return kv_copy(kv_all.at[origin, 1], origin, 1, peer, relay_sem.at[0])
+        return kv_copy(kv_all.at[origin, which], origin, which, peer, relay_sem.at[which])
 
     def pass_on(step, which):
         low, high = level - step, level + step
@@ -268,11 +274,11 @@
 
     def across(lev, which):
         arrived(index(lev, 1 - side, core), which)
-        if which == 1 and lev is level:
+        if which >= groups and lev is level:
 
             @pl.when(relieved)
             def _():
-                to_paired().start()
+                to_paired(which).start()
 
         to_c(lev, 1 - side, which, False).start()
 
@@ -297,33 +303,6 @@
         def _(pair):
             move(pair)
 
-    def pass_core_or_own(step, which):
-        @pl.when(step == 0)
-        def _():
-            across(level, which)
-
-        @pl.when(step > 0)
-        def _():
-            pass_core(step, which)
-
-    pass_on(1, 0)
-    across(level, 0)
-    moves(1)
-
-    @pl.loop(2, tall)
-    def _(step):
-        pass_on(step, 0)
-        pass_core(step - 1, 0)
-        pass_on(step - 1, 1)
-        pass_core_or_own(step - 2, 1)
-        moves(step)
-
-    pass_core(tall - 1, 0)
-    own_copy(0).wait()
-    own_copy(2).wait()
-    y_copy(0).wait_recv()
-    from_core(0)
-
     def head_columns(pair, i):
         return pl.ds(pl.multiple_of(pair * wide + i * HD, HD), HD)
 
@@ -335,81 +314,108 @@
         for i in range(grouped):
             head = group * grouped + i
             at = pl.ds(pl.multiple_of(head * HD, HD), HD)
-            scores = rows_by_rows(joined(q_all[:, :, at]), joined(kv_all[:, 0, :, at]))
+            scores = rows_by_rows(joined(q_all[:, :, at]), joined(kv_all[:, group, :, i * HD : (i + 1) * HD]))
             peak = jnp.max(scores, axis=1, keepdims=True)
             weights = jnp.exp((scores - peak) * scale)
             total = jnp.sum(weights, axis=1, keepdims=True)
             probs[head] = weights.astype(jnp.bfloat16)
             totals[head] = jnp.broadcast_to(total, (2 * rows, HD))
 
-    weigh(0)
-    pass_on(tall - 1, 1)
-    pass_core_or_own(tall - 2, 1)
-
-    @pl.loop(1, groups)
-    def _(group):
-        weigh(group)
-
-    pass_core(tall - 1, 1)
-    own_copy(1).wait()
-    own_copy(3).wait()
-    y_copy(1).wait_recv()
-    from_core(1)
-
-    def span(which, part):
-        size = (grouped * HD, wide)[which]
-        return pl.multiple_of(part * size, HD), size
-
-    def back_copy(which, part):
+    def span(which, piece):
+        size = (part, wide)[which]
+        return pl.multiple_of(piece * size, HD), size
+
+    def back_copy(which, piece):
         source, target = ((att, att_ref), (out, out_ref))[which]
-        start, size = span(which, part)
+        start, size = span(which, piece)
         return pltpu.make_async_remote_copy(
             src_ref=source.at[other, :, pl.ds(start, size)],
             dst_ref=target.at[:, pl.ds(pl.multiple_of(mine + start, HD), size)],
-            send_sem=back_send.at[which, part],
-            recv_sem=back_recv.at[which, part],
+            send_sem=back_send.at[which, piece],
+            recv_sem=back_recv.at[which, piece],
             device_id=(me, other),
             device_id_type=MESH,
         )
 
-    def own_out(which, part):
+    def own_out(which, piece):
         source, target = ((att, att_ref), (out, out_ref))[which]
-        start, size = span(which, part)
+        start, size = span(which, piece)
         return pltpu.make_async_copy(
             source.at[branch, :, pl.ds(start, size)],
             target.at[:, pl.ds(pl.multiple_of(mine + start, HD), size)],
-            own_out_sem.at[which, part],
+            own_out_sem.at[which, piece],
         )
 
-    squares[0] = jnp.zeros((2 * rows, HD), jnp.float32)
-
-    @pl.loop(0, groups)
-    def _(group):
-        added = squares[0]
+    tall_rows = squares.shape[0]
+    squares[...] = jnp.zeros((tall_rows, HD), jnp.float32)
+
+    def attend(group):
+        added = squares[0 : 2 * rows, :]
         for i in range(grouped):
             head = group * grouped + i
-            at = pl.ds(pl.multiple_of(head * HD, HD), HD)
-            summed = jnp.dot(
-                probs[head],
-                joined(kv_all[:, 1, :, at]),
-                preferred_element_type=jnp.float32,
-            )
+            at = slice(head * HD, (head + 1) * HD)
+            values = joined(kv_all[:, groups + group, :, i * HD : (i + 1) * HD])
+            summed = jnp.dot(probs[head], values, preferred_element_type=jnp.float32)
             rounded = (summed / totals[head]).reshape(2, rows, HD).astype(jnp.bfloat16)
             att[:, :, at] = rounded
             middle = r_all[:, :, at].astype(jnp.float32) + rounded.astype(jnp.float32)
             mid[:, :, at] = middle
             middle = middle.reshape(2 * rows, HD)
             added = added + middle * middle
-        squares[0] = added
+        squares[0 : 2 * rows, :] = added
         back_copy(0, group).start()
         own_out(0, group).start()
 
-    squares[0] = jnp.broadcast_to(
-        jnp.sum(squares[0], axis=1, keepdims=True), (2 * rows, HD)
-    )
+    @pl.loop(1, tall + classes)
+    def _(turn):
+        for which in range(classes):
+            step = turn - which
+
+            @pl.when(jnp.logical_and(step >= 1, step < tall))
+            def _():
+                pass_on(step, which)
+
+            @pl.when(step == 1)
+            def _():
+                across(level, which)
+
+            @pl.when(jnp.logical_and(step >= 2, step <= tall))
+            def _():
+                pass_core(step - 1, which)
+
+        @pl.when(turn < tall)
+        def _():
+            moves(turn)
+
+        for which in range(classes - 1):
+
+            @pl.when(turn == tall + which)
+            def _():
+                if which == 0:
+                    own_copy(0).wait()
+                    y_copy(0).wait_recv()
+                if which == groups:
+                    own_copy(1).wait()
+                    y_copy(1).wait_recv()
+                own_copy(2 + which).wait()
+                from_core(which)
+                if which < groups:
+                    weigh(which)
+                else:
+                    attend(which - groups)
+
+    if groups == 1:
+        own_copy(1).wait()
+        y_copy(1).wait_recv()
+    own_copy(1 + classes).wait()
+    from_core(classes - 1)
+    attend(groups - 1)
+
+    lanes = jnp.sum(squares[...].T, axis=0, keepdims=True)
+    partial[0] = jnp.broadcast_to(lanes, (8, tall_rows))
     square_copy = pltpu.make_async_remote_copy(
-        src_ref=squares.at[0],
-        dst_ref=squares.at[1],
+        src_ref=partial.at[0],
+        dst_ref=partial.at[1],
         send_sem=y_send.at[2],
         recv_sem=y_recv.at[2],
         device_id=(me, other),
@@ -417,8 +423,8 @@
     )
     square_copy.start()
     square_copy.wait_recv()
-    norm = lax.rsqrt((squares[0] + squares[1]) * (1.0 / (2 * half)) + 1e-06)
-    squares[2] = norm
+    norm = lax.rsqrt((partial[0, 0:1] + partial[1, 0:1]) * (1.0 / (2 * half)) + 1e-06)
+    squares[...] = jnp.broadcast_to(norm, (HD, tall_rows)).T
 
     def text_map(query, keys):
         scores = rows_by_rows(query, keys)
@@ -431,7 +437,7 @@
             at = head_columns(pair, i)
             gain = gain_ref[:, pl.ds(pl.multiple_of(mine + pair * wide + i * HD, HD), HD)]
             middle = mid[:, :, at]
-            query = middle.reshape(2 * rows, HD) * squares[2] * gain.astype(jnp.float32)
+            query = middle.reshape(2 * rows, HD) * squares[0 : 2 * rows, :] * gain.astype(jnp.float32)
             query = query.reshape(2, rows, HD).astype(jnp.bfloat16)
             source_map = text_map(query[0], text[0, :, at])
             edit_map = text_map(query[1], moved[0, :, at])
@@ -454,21 +460,19 @@
     for which in range(2):
 
         @pl.loop(0, (groups, pairs)[which])
-        def _(part):
-            back_copy(which, part).wait()
-            own_out(which, part).wait()
+        def _(piece):
+            back_copy(which, piece).wait()
+            own_out(which, piece).wait()
 
         y_copy(which).wait_send()
+
+    for which in range(classes):
 
         @pl.loop(0, tall)
         def _(lev):
-            if which == 0:
+            @pl.when(jnp.logical_not(relayed(lev, which)))
+            def _():
                 to_x(lev, which, False).wait_send()
-            else:
-
-                @pl.when(jnp.logical_not(relayed(lev, which)))
-                def _():
-                    to_x(lev, which, False).wait_send()
 
             to_c(lev, 0, which, False).wait_send()
             to_c(lev, 1, which, False).wait_send()
@@ -481,9 +485,11 @@
             def _():
                 to_below(lev, which, False).wait_send()
 
-    @pl.when(relieved)
-    def _():
-        to_paired().wait_send()
+        if which >= groups:
+
+            @pl.when(relieved)
+            def _():
+                to_paired(which).wait_send()
 
     square_copy.wait_send()
 
@@ -501,6 +507,9 @@
     text_len = word_align.shape[0]
     keys = n * rows
     tall = n // 4
+    grouped = heads // 2 if heads % 2 == 0 else heads
+    classes = 2 * heads // grouped
+    tall_rows = pl.cdiv(2 * rows, HD) * HD
     vmem = pl.BlockSpec(memory_space=pltpu.VMEM)
     hbm = pl.BlockSpec(memory_space=pl.ANY)
     shape = jax.ShapeDtypeStruct((rows, width), jnp.bfloat16)
@@ -509,12 +518,12 @@
     attended, result = pl.pallas_call(
         functools.partial(kernel, n),
         out_shape=(shape, shape),
-        in_specs=[vmem, vmem, vmem, vmem, hbm, vmem, vmem],
+        in_specs=[hbm, hbm, hbm, vmem, hbm, vmem, vmem],
         out_specs=(hbm, hbm),
         scratch_shapes=[
             pltpu.VMEM((2, rows, half), bf16),
             pltpu.VMEM((2, rows, half), bf16),
-            pltpu.VMEM((n, 2, rows, half), bf16),
+            pltpu.VMEM((n, classes, rows, grouped * HD), bf16),
             pltpu.VMEM((4, text_len, half), bf16),
             pltpu.VMEM((2, text_len, half), bf16),
             pltpu.VMEM((text_len, text_len), bf16),
@@ -522,17 +531,18 @@
             pltpu.VMEM((heads, 2 * rows, HD), f32),
             pltpu.VMEM((2, rows, half), bf16),
             pltpu.VMEM((2, rows, half), f32),
-            pltpu.VMEM((3, 2 * rows, HD), f32),
+            pltpu.VMEM((tall_rows, HD), f32),
+            pltpu.VMEM((2, 8, tall_rows), f32),
             pltpu.VMEM((2, rows, half), bf16),
             dma((4,)),
-            dma((4,)),
+            dma((2 + classes,)),
             dma((2, pairs)),
-            dma((n, 2)),
-            dma((tall, 2)),
-            dma((tall, 2)),
-            dma((tall, 2)),
-            dma((2 * tall, 2)),
-            dma((1,)),
+            dma((n, classes)),
+            dma((tall, classes)),
+            dma((tall, classes)),
+            dma((tall, classes)),
+            dma((2 * tall, classes)),
+            dma((classes,)),
             dma((3,)),
             dma((3,)),
             dma((2, pairs)),

time: 56.2 us -> 54.5 us (0.970)
  Pallas kernels: 54.1 us -> 52.3 us
    pallas_call x1, Pallas kernels: 52.2 us -> 50.4 us  [per_device(): pl.pallas_call(functools.partial(kernel, n), out_shape=(shape, shape), in...]
where the time goes in v4:
time: 54.5 us; the launch traced here: 54.2 us
  Pallas kernels  52.3 us (96%)
  local copies, waits for them, and re-layouts  1.3 us (2%)
  between operations  0.64 us (1%)
    pallas_call x1, Pallas kernels, per_device(): pl.pallas_call(functools.partial(kernel, n), out_shape=(shape, shape), in...  50.4 us
    pallas_call x1, Pallas kernels, per_device(): pl.pallas_call(copy_out, out_shape=(shape, shape), in_specs=[vmem, vmem],...  1.87 us
    broadcast_in_dim x1, local copies, waits for them, and re-layouts, per_device(): cross_gain[None]  1.3 us

profile of v4, /device:TPU:0, one launch (start us, length us, event | category | flops | bytes accessed | tf_op | source)
XLA Modules:
  0.0 54.2 jit_solution(5496281553728252489)
XLA Ops:
  0.6 1.3 %broadcast_in_dim.12.gain_ref = bf16[1,2560]{1,0:T(2,128)(2,1)} reshape(bf16[2560]{0:T(1024)(128)(2,1)} %param.10) | data formatting | bytes 10240 | tf_op jit(solution)/shard_map/broadcast_in_dim | solution.py:558
  1.9 50.4 %shard_map.86 = (bf16[56,2560]{1,0:T(8,128)(2,1)}, bf16[56,2560]{1,0:T(8,128)(2,1)}) custom-call(bf16[56,2560]{1,0:T(8,128)(2,1)} %bitcast.5, bf16[2,56,1280]{2,1,0:T(8,128)(2,1)} %kv_ref.1, bf16[56,2560]{1,0:T(8,128)(2,1)} %bitcast.6, bf16[1,2560]{1,0:T(2,128)(2,1)} %broadcast_in_dim.12.gain_ref, bf16[2,2,512,2560]{3,2,1,0:T(8,128)(2,1)} %text_ref.1, ...), custom_call_target="tpu_custom_call" | custom-call | tf_op jit(solution)/shard_map/pallas_call | solution.py:518
  52.3 1.9 %shard_map.87 = (bf16[56,2560]{1,0:T(8,128)(2,1)}, bf16[56,2560]{1,0:T(8,128)(2,1)}) custom-call(bf16[56,2560]{1,0:T(8,128)(2,1)} %get-tuple-element.6.att_in, bf16[56,2560]{1,0:T(8,128)(2,1)} %get-tuple-element.7.out_in), custom_call_target="tpu_custom_call" | custom-call | tf_op jit(solution)/shard_map/pallas_call | solution.py:563

commit v5 on v4

--- a/solution.py
+++ b/solution.py
@@ -42,6 +42,7 @@
     mid,
     squares,
     partial,
+    gains,
     out,
     text_sem,
     own_sem,
@@ -142,25 +143,21 @@
             device_id_type=MESH,
         )
 
-    def to_above(lev, which, own):
+    def to_above(lev, which):
         origin = index(lev, side, core)
-        source = own_kv(which) if own else kv_all.at[origin, which]
-        return kv_copy(source, origin, which, above, send_up.at[lev, which])
-
-    def to_below(lev, which, own):
+        return kv_copy(kv_all.at[origin, which], origin, which, above, send_up.at[lev, which])
+
+    def to_below(lev, which):
         origin = index(lev, side, core)
-        source = own_kv(which) if own else kv_all.at[origin, which]
-        return kv_copy(source, origin, which, below, send_down.at[lev, which])
-
-    def to_x(lev, which, own):
+        return kv_copy(kv_all.at[origin, which], origin, which, below, send_down.at[lev, which])
+
+    def to_x(lev, which):
         origin = index(lev, side, core)
-        source = own_kv(which) if own else kv_all.at[origin, which]
-        return kv_copy(source, origin, which, x_peer, send_x.at[lev, which])
-
-    def to_c(lev, sid, which, own):
+        return kv_copy(kv_all.at[origin, which], origin, which, x_peer, send_x.at[lev, which])
+
+    def to_c(lev, sid, which):
         origin = index(lev, sid, core)
-        source = own_kv(which) if own else kv_all.at[origin, which]
-        return kv_copy(source, origin, which, c_peer, send_c.at[lev * 2 + sid, which])
+        return kv_copy(kv_all.at[origin, which], origin, which, c_peer, send_c.at[lev * 2 + sid, which])
 
     def arrived(origin, which):
         pltpu.make_async_remote_copy(
@@ -184,23 +181,25 @@
         )
 
     def send_own(which):
-        to_x(level, which, True).start()
+        to_x(level, which).start()
 
         @pl.when(has_above)
         def _():
-            to_above(level, which, True).start()
+            to_above(level, which).start()
 
         @pl.when(has_below)
         def _():
-            to_below(level, which, True).start()
-
-        to_c(level, side, which, True).start()
+            to_below(level, which).start()
+
+        to_c(level, side, which).start()
 
     for which in range(classes):
+        own_copy(2 + which).wait()
         send_own(which)
         if which < 2:
             y_copy(which).start()
 
+    gains[...] = gain_ref[...].astype(jnp.float32).reshape(1, 2 * half)
     align = align_ref[...]
     chosen = lax.broadcasted_iota(jnp.int32, (text_len, text_len), 0) == align
     place[...] = jnp.where(chosen, 1.0, 0.0).astype(jnp.bfloat16)
@@ -235,12 +234,12 @@
 
     def forward_x(lev, which):
         if which < groups:
-            to_x(lev, which, False).start()
+            to_x(lev, which).start()
         else:
 
             @pl.when(jnp.logical_not(relayed(lev, which)))
             def _():
-                to_x(lev, which, False).start()
+                to_x(lev, which).start()
 
     def to_paired(which):
         origin = index(level, 1 - side, core)
@@ -256,10 +255,10 @@
 
             @pl.when(has_above)
             def _():
-                to_above(low, which, False).start()
+                to_above(low, which).start()
 
             forward_x(low, which)
-            to_c(low, side, which, False).start()
+            to_c(low, side, which).start()
 
         @pl.when(high < tall)
         def _():
@@ -267,10 +266,10 @@
 
             @pl.when(has_below)
             def _():
-                to_below(high, which, False).start()
+                to_below(high, which).start()
 
             forward_x(high, which)
-            to_c(high, side, which, False).start()
+            to_c(high, side, which).start()
 
     def across(lev, which):
         arrived(index(lev, 1 - side, core), which)
@@ -280,7 +279,7 @@
             def _():
                 to_paired(which).start()
 
-        to_c(lev, 1 - side, which, False).start()
+        to_c(lev, 1 - side, which).start()
 
     def pass_core(step, which):
         low, high = level - step, level + step
@@ -366,50 +365,46 @@
         back_copy(0, group).start()
         own_out(0, group).start()
 
-    @pl.loop(1, tall + classes)
-    def _(turn):
+    def compute(which):
+        if which == 0:
+            own_copy(0).wait()
+            y_copy(0).wait_recv()
+        if which == groups:
+            own_copy(1).wait()
+            y_copy(1).wait_recv()
+        from_core(which)
+        if which < groups:
+            weigh(which)
+        else:
+            attend(which - groups)
+
+    @pl.loop(1, tall - 1)
+    def _(step):
         for which in range(classes):
-            step = turn - which
-
-            @pl.when(jnp.logical_and(step >= 1, step < tall))
-            def _():
-                pass_on(step, which)
+            pass_on(step, which)
 
             @pl.when(step == 1)
             def _():
                 across(level, which)
 
-            @pl.when(jnp.logical_and(step >= 2, step <= tall))
+            @pl.when(step > 1)
             def _():
                 pass_core(step - 1, which)
 
-        @pl.when(turn < tall)
-        def _():
-            moves(turn)
-
-        for which in range(classes - 1):
-
-            @pl.when(turn == tall + which)
-            def _():
-                if which == 0:
-                    own_copy(0).wait()
-                    y_copy(0).wait_recv()
-                if which == groups:
-                    own_copy(1).wait()
-                    y_copy(1).wait_recv()
-                own_copy(2 + which).wait()
-                from_core(which)
-                if which < groups:
-                    weigh(which)
-                else:
-                    attend(which - groups)
-
-    if groups == 1:
-        own_copy(1).wait()
-        y_copy(1).wait_recv()
-    own_copy(1 + classes).wait()
-    from_core(classes - 1)
-    attend(groups - 1)
+        moves(step)
+
+    moves(tall - 1)
+    for which in range(classes):
+        pass_on(tall - 1, which)
+        if tall == 2:
+            across(level, which)
+        else:
+            pass_core(tall - 2, which)
+        if which > 0:
+            pass_core(tall - 1, which - 1)
+            compute(which - 1)
+    pass_core(tall - 1, classes - 1)
+    compute(classes - 1)
 
     lanes = jnp.sum(squares[...].T, axis=0, keepdims=True)
     partial[0] = jnp.broadcast_to(lanes, (8, tall_rows))
@@ -435,9 +430,9 @@
     def _(pair):
         for i in range(PAIR):
             at = head_columns(pair, i)
-            gain = gain_ref[:, pl.ds(pl.multiple_of(mine + pair * wide + i * HD, HD), HD)]
+            gain = gains[:, pl.ds(pl.multiple_of(mine + pair * wide + i * HD, HD), HD)]
             middle = mid[:, :, at]
-            query = middle.reshape(2 * rows, HD) * squares[0 : 2 * rows, :] * gain.astype(jnp.float32)
+            query = middle.reshape(2 * rows, HD) * squares[0 : 2 * rows, :] * gain
             query = query.reshape(2, rows, HD).astype(jnp.bfloat16)
             source_map = text_map(query[0], text[0, :, at])
             edit_map = text_map(query[1], moved[0, :, at])
@@ -472,18 +467,18 @@
         def _(lev):
             @pl.when(jnp.logical_not(relayed(lev, which)))
             def _():
-                to_x(lev, which, False).wait_send()
-
-            to_c(lev, 0, which, False).wait_send()
-            to_c(lev, 1, which, False).wait_send()
+                to_x(lev, which).wait_send()
+
+            to_c(lev, 0, which).wait_send()
+            to_c(lev, 1, which).wait_send()
 
             @pl.when(jnp.logical_and(has_above, lev <= level))
             def _():
-                to_above(lev, which, False).wait_send()
+                to_above(lev, which).wait_send()
 
             @pl.when(jnp.logical_and(has_below, lev >= level))
             def _():
-                to_below(lev, which, False).wait_send()
+                to_below(lev, which).wait_send()
 
         if which >= groups:
 
@@ -533,6 +528,7 @@
             pltpu.VMEM((2, rows, half), f32),
             pltpu.VMEM((tall_rows, HD), f32),
             pltpu.VMEM((2, 8, tall_rows), f32),
+            pltpu.VMEM((1, width), f32),
             pltpu.VMEM((2, rows, half), bf16),
             dma((4,)),
             dma((2 + classes,)),
@@ -555,7 +551,7 @@
         queries[0],
         keys_values,
         residual_in[0],
-        cross_gain[None],
+        cross_gain,
         text_kv,
         prompt_ids,
         word_align[None],

time: 54.5 us -> 51.2 us (0.939)
  Pallas kernels: 52.3 us -> 50.3 us
  local copies, waits for them, and re-layouts: 1.3 us -> 0 us
    pallas_call x1, Pallas kernels: 50.4 us -> 48.5 us  [per_device(): pl.pallas_call(functools.partial(kernel, n), out_shape=(shape, shape), in...]
    broadcast_in_dim x1 -> x0, local copies, waits for them, and re-layouts: 1.3 us -> none  [per_device(): cross_gain[None]]
where the time goes in v5:
time: 51.2 us; the launch traced here: 51 us
  Pallas kernels  50.3 us (98%)
  between operations  0.64 us (1%)
    pallas_call x1, Pallas kernels, per_device(): pl.pallas_call(functools.partial(kernel, n), out_shape=(shape, shape), in...  48.5 us
    pallas_call x1, Pallas kernels, per_device(): pl.pallas_call(copy_out, out_shape=(shape, shape), in_specs=[vmem, vmem],...  1.87 us

profile of v5, /device:TPU:0, one launch (start us, length us, event | category | flops | bytes accessed | tf_op | source)
XLA Modules:
  0.0 51.0 jit_solution(17705585903712055661)
XLA Ops:
  0.6 48.5 %shard_map.86 = (bf16[56,2560]{1,0:T(8,128)(2,1)}, bf16[56,2560]{1,0:T(8,128)(2,1)}) custom-call(bf16[56,2560]{1,0:T(8,128)(2,1)} %bitcast.5, bf16[2,56,1280]{2,1,0:T(8,128)(2,1)} %kv_ref.1, bf16[56,2560]{1,0:T(8,128)(2,1)} %bitcast.6, bf16[2560]{0:T(1024)(128)(2,1)} %gain_ref.1, bf16[2,2,512,2560]{3,2,1,0:T(8,128)(2,1)} %text_ref.1, s32[2,512]{1,0:T(2,128)} %ids_ref.1, ...), custom_call_target="tpu_custom_call" | custom-call | tf_op jit(solution)/shard_map/pallas_call | solution.py:513
  49.1 1.9 %shard_map.87 = (bf16[56,2560]{1,0:T(8,128)(2,1)}, bf16[56,2560]{1,0:T(8,128)(2,1)}) custom-call(bf16[56,2560]{1,0:T(8,128)(2,1)} %get-tuple-element.6.att_in, bf16[56,2560]{1,0:T(8,128)(2,1)} %get-tuple-element.7.out_in), custom_call_target="tpu_custom_call" | custom-call | tf_op jit(solution)/shard_map/pallas_call | solution.py:559

commit v6 on v5

--- a/solution.py
+++ b/solution.py
@@ -93,9 +93,6 @@
             text_ref.at[i // 2, i % 2, :, pl.ds(mine, half)], text.at[i], text_sem.at[i]
         )
 
-    for i in range(4):
-        text_copy(i).start()
-
     def own_copy(i):
         if i == 0:
             return pltpu.make_async_copy(
@@ -107,8 +104,10 @@
             )
         return pltpu.make_async_copy(own_kv(i - 2), kv_all.at[me, i - 2], own_sem.at[i])
 
-    for i in range(2 + classes):
+    for i in (*range(2, 2 + classes), 0, 1):
         own_copy(i).start()
+    for i in (1, 3, 0, 2):
+        text_copy(i).start()
 
     barrier = pltpu.get_barrier_semaphore()
 
@@ -318,7 +317,7 @@
             weights = jnp.exp((scores - peak) * scale)
             total = jnp.sum(weights, axis=1, keepdims=True)
             probs[head] = weights.astype(jnp.bfloat16)
-            totals[head] = jnp.broadcast_to(total, (2 * rows, HD))
+            totals[head] = jnp.broadcast_to(1.0 / total, (2 * rows, HD))
 
     def span(which, piece):
         size = (part, wide)[which]
@@ -355,7 +354,7 @@
             at = slice(head * HD, (head + 1) * HD)
             values = joined(kv_all[:, groups + group, :, i * HD : (i + 1) * HD])
             summed = jnp.dot(probs[head], values, preferred_element_type=jnp.float32)
-            rounded = (summed / totals[head]).reshape(2, rows, HD).astype(jnp.bfloat16)
+            rounded = (summed * totals[head]).reshape(2, rows, HD).astype(jnp.bfloat16)
             att[:, :, at] = rounded
             middle = r_all[:, :, at].astype(jnp.float32) + rounded.astype(jnp.float32)
             mid[:, :, at] = middle
@@ -424,7 +423,7 @@
     def text_map(query, keys):
         scores = rows_by_rows(query, keys)
         weights = jnp.exp((scores - jnp.max(scores, axis=1, keepdims=True)) * scale)
-        return weights / jnp.sum(weights, axis=1, keepdims=True)
+        return weights * (1.0 / jnp.sum(weights, axis=1, keepdims=True))
 
     @pl.loop(0, pairs)
     def _(pair):
@@ -489,9 +488,15 @@
     square_copy.wait_send()
 
 
-def copy_out(att_in, out_in, att_ref, out_ref):
-    att_ref[...] = att_in[...]
-    out_ref[...] = out_in[...]
+def copy_out(att_in, out_in, att_ref, out_ref, sem):
+    copies = (
+        pltpu.make_async_copy(att_in, att_ref, sem.at[0]),
+        pltpu.make_async_copy(out_in, out_ref, sem.at[1]),
+    )
+    for copy in copies:
+        copy.start()
+    for copy in copies:
+        copy.wait()
 
 
 def per_device(n, queries, keys_values, residual_in, cross_gain, text_kv, prompt_ids, word_align):
@@ -512,9 +517,9 @@
     dma = pltpu.SemaphoreType.DMA
     attended, result = pl.pallas_call(
         functools.partial(kernel, n),
-        out_shape=(shape, shape),
+        out_shape=(pltpu.VMEM((rows, width), bf16), pltpu.VMEM((rows, width), bf16)),
         in_specs=[hbm, hbm, hbm, vmem, hbm, vmem, vmem],
-        out_specs=(hbm, hbm),
+        out_specs=(vmem, vmem),
         scratch_shapes=[
             pltpu.VMEM((2, rows, half), bf16),
             pltpu.VMEM((2, rows, half), bf16),
@@ -560,7 +565,8 @@
         copy_out,
         out_shape=(shape, shape),
         in_specs=[vmem, vmem],
-        out_specs=(vmem, vmem),
+        out_specs=(hbm, hbm),
+        scratch_shapes=[dma((2,))],
     )(attended, result)
     return (attended[None], result[None])
 

time: 51.2 us -> 52.5 us (1.025)
  local copies, waits for them, and re-layouts: 0 us -> 1.41 us
    unnamed x0 -> x4, local copies, waits for them, and re-layouts: none -> 1.41 us
where the time goes in v6:
time: 52.5 us; the launch traced here: 52.3 us
  Pallas kernels  50.3 us (96%)
  local copies, waits for them, and re-layouts  1.41 us (3%)
  between operations  0.65 us (1%)
    pallas_call x1, Pallas kernels, per_device(): pl.pallas_call(functools.partial(kernel, n), out_shape=(pltpu.VMEM((rows,...  48.4 us
    pallas_call x1, Pallas kernels, per_device(): pl.pallas_call(copy_out, out_shape=(shape, shape), in_specs=[vmem, vmem],...  1.87 us
    unnamed x4, local copies, waits for them, and re-layouts  1.41 us

profile of v6, /device:TPU:0, one launch (start us, length us, event | category | flops | bytes accessed | tf_op | source)
XLA Modules:
  0.0 52.3 jit_solution(15565364351532268407)
XLA Ops:
  0.6 48.4 %shard_map.86 = (bf16[56,2560]{1,0:T(8,128)(2,1)S(1)}, bf16[56,2560]{1,0:T(8,128)(2,1)S(1)}) custom-call(bf16[56,2560]{1,0:T(8,128)(2,1)} %bitcast.5, bf16[2,56,1280]{2,1,0:T(8,128)(2,1)} %kv_ref.1, bf16[56,2560]{1,0:T(8,128)(2,1)} %bitcast.6, bf16[2560]{0:T(1024)(128)(2,1)} %gain_ref.1, bf16[2,2,512,2560]{3,2,1,0:T(8,128)(2,1)} %text_ref.1, ...), custom_call_target="tpu_custom_call" | custom-call | tf_op jit(solution)/shard_map/pallas_call | solution.py:518
  49.1 0.0 copy-start
  49.1 0.7 %copy-done = bf16[56,2560]{1,0:T(8,128)(2,1)} copy-done((bf16[56,2560]{1,0:T(8,128)(2,1)}, bf16[56,2560]{1,0:T(8,128)(2,1)S(1)}, u32[]{:S(2)}) %copy-start) | copy-done | bytes 286744
  49.8 0.0 copy-start.1
  49.8 0.7 %copy-done.1 = bf16[56,2560]{1,0:T(8,128)(2,1)} copy-done((bf16[56,2560]{1,0:T(8,128)(2,1)}, bf16[56,2560]{1,0:T(8,128)(2,1)S(1)}, u32[]{:S(2)}) %copy-start.1) | copy-done | bytes 286744
  50.5 1.9 %shard_map.87 = (bf16[56,2560]{1,0:T(8,128)(2,1)}, bf16[56,2560]{1,0:T(8,128)(2,1)}) custom-call(bf16[56,2560]{1,0:T(8,128)(2,1)} %copy-done, bf16[56,2560]{1,0:T(8,128)(2,1)} %copy-done.1), custom_call_target="tpu_custom_call" | custom-call | tf_op jit(solution)/shard_map/pallas_call | solution.py:564
Async XLA Ops:
  49.1 0.7 %copy-start = (bf16[56,2560]{1,0:T(8,128)(2,1)}, bf16[56,2560]{1,0:T(8,128)(2,1)S(1)}, u32[]{:S(2)}) copy-start(bf16[56,2560]{1,0:T(8,128)(2,1)S(1)} %get-tuple-element.6.att_in) | copy-start | bytes 860164
  49.8 0.7 %copy-start.1 = (bf16[56,2560]{1,0:T(8,128)(2,1)}, bf16[56,2560]{1,0:T(8,128)(2,1)S(1)}, u32[]{:S(2)}) copy-start(bf16[56,2560]{1,0:T(8,128)(2,1)S(1)} %get-tuple-element.7.out_in) | copy-start | bytes 860164

commit v7 on v6

--- a/solution.py
+++ b/solution.py
@@ -10,6 +10,7 @@
 
 HD = 128
 PAIR = 2
+CHUNK = 4
 MESH = pl.DeviceIdType.MESH
 
 
@@ -67,6 +68,7 @@
     groups = heads // grouped
     part = grouped * HD
     classes = 2 * groups
+    chunks = pl.cdiv(heads, CHUNK)
     text_len = text_ref.shape[2]
     tall = n // 4
     scale = 1.0 / math.sqrt(HD)
@@ -301,9 +303,6 @@
         def _(pair):
             move(pair)
 
-    def head_columns(pair, i):
-        return pl.ds(pl.multiple_of(pair * wide + i * HD, HD), HD)
-
     def joined(value):
         flat = value.astype(jnp.float32).reshape(value.shape[0] * value.shape[1], HD)
         return flat.astype(jnp.bfloat16)
@@ -320,8 +319,9 @@
             totals[head] = jnp.broadcast_to(1.0 / total, (2 * rows, HD))
 
     def span(which, piece):
-        size = (part, wide)[which]
-        return pl.multiple_of(piece * size, HD), size
+        if which == 0:
+            return piece * part, part
+        return piece * CHUNK * HD, min(CHUNK, heads - piece * CHUNK) * HD
 
     def back_copy(which, piece):
         source, target = ((att, att_ref), (out, out_ref))[which]
@@ -425,11 +425,10 @@
         weights = jnp.exp((scores - jnp.max(scores, axis=1, keepdims=True)) * scale)
         return weights * (1.0 / jnp.sum(weights, axis=1, keepdims=True))
 
-    @pl.loop(0, pairs)
-    def _(pair):
-        for i in range(PAIR):
-            at = head_columns(pair, i)
-            gain = gains[:, pl.ds(pl.multiple_of(mine + pair * wide + i * HD, HD), HD)]
+    for chunk in range(chunks):
+        for head in range(chunk * CHUNK, min(heads, (chunk + 1) * CHUNK)):
+            at = slice(head * HD, (head + 1) * HD)
+            gain = gains[:, pl.ds(pl.multiple_of(mine + head * HD, HD), HD)]
             middle = mid[:, :, at]
             query = middle.reshape(2 * rows, HD) * squares[0 : 2 * rows, :] * gain
             query = query.reshape(2, rows, HD).astype(jnp.bfloat16)
@@ -448,13 +447,12 @@
             )
             out[0, :, at] = (middle[0] + source_out).astype(jnp.bfloat16)
             out[1, :, at] = (middle[1] + edit_out).astype(jnp.bfloat16)
-        back_copy(1, pair).start()
-        own_out(1, pair).start()
+        back_copy(1, chunk).start()
+        own_out(1, chunk).start()
 
     for which in range(2):
 
-        @pl.loop(0, (groups, pairs)[which])
-        def _(piece):
+        for piece in range((groups, chunks)[which]):
             back_copy(which, piece).wait()
             own_out(which, piece).wait()
 
@@ -486,17 +484,6 @@
                 to_paired(which).wait_send()
 
     square_copy.wait_send()
-
-
-def copy_out(att_in, out_in, att_ref, out_ref, sem):
-    copies = (
-        pltpu.make_async_copy(att_in, att_ref, sem.at[0]),
-        pltpu.make_async_copy(out_in, out_ref, sem.at[1]),
-    )
-    for copy in copies:
-        copy.start()
-    for copy in copies:
-        copy.wait()
 
 
 def per_device(n, queries, keys_values, residual_in, cross_gain, text_kv, prompt_ids, word_align):
@@ -561,13 +548,6 @@
         prompt_ids,
         word_align[None],
     )
-    attended, result = pl.pallas_call(
-        copy_out,
-        out_shape=(shape, shape),
-        in_specs=[vmem, vmem],
-        out_specs=(hbm, hbm),
-        scratch_shapes=[dma((2,))],
-    )(attended, result)
     return (attended[None], result[None])
 
 

time: 52.5 us -> 50.6 us (0.964)
  Pallas kernels: 50.3 us -> 48.3 us
    pallas_call x1 -> x0, Pallas kernels: 1.87 us -> none  [per_device(): pl.pallas_call(copy_out, out_shape=(shape, shape), in_specs=[vmem, vmem],...]
    unnamed x4 -> x2, local copies, waits for them, and re-layouts: 1.41 us -> 1.42 us
where the time goes in v7:
time: 50.6 us; the launch traced here: 50.4 us
  Pallas kernels  48.3 us (95%)
  local copies, waits for them, and re-layouts  1.42 us (3%)
  between operations  0.64 us (1%)
    pallas_call x1, Pallas kernels, per_device(): pl.pallas_call(functools.partial(kernel, n), out_shape=(pltpu.VMEM((rows,...  48.3 us
    unnamed x2, local copies, waits for them, and re-layouts  1.42 us

profile of v7, /device:TPU:0, one launch (start us, length us, event | category | flops | bytes accessed | tf_op | source)
XLA Modules:
  0.0 50.4 jit_solution(7732962442518271550)
XLA Ops:
  0.6 48.3 %shard_map.86 = (bf16[56,2560]{1,0:T(8,128)(2,1)S(1)}, bf16[56,2560]{1,0:T(8,128)(2,1)S(1)}) custom-call(bf16[56,2560]{1,0:T(8,128)(2,1)} %bitcast.7, bf16[2,56,1280]{2,1,0:T(8,128)(2,1)} %kv_ref.1, bf16[56,2560]{1,0:T(8,128)(2,1)} %bitcast.8, bf16[2560]{0:T(1024)(128)(2,1)} %gain_ref.1, bf16[2,2,512,2560]{3,2,1,0:T(8,128)(2,1)} %text_ref.1, ...), custom_call_target="tpu_custom_call" | custom-call | tf_op jit(solution)/shard_map/pallas_call | solution.py:505
  48.9 0.7 %copy.11 = bf16[1,56,2560]{2,1,0:T(8,128)(2,1)} copy(bf16[1,56,2560]{2,1,0:T(8,128)(2,1)S(1)} %bitcast.6) | data formatting | bytes 573440
  49.7 0.7 %copy.12 = bf16[1,56,2560]{2,1,0:T(8,128)(2,1)} copy(bf16[1,56,2560]{2,1,0:T(8,128)(2,1)S(1)} %bitcast.5) | data formatting | bytes 573440
